TPU v7x, 256 devices: a whole 4x4x8 slice. The times are simulated.
256 devices in a mesh: freq: 8 (over x, z_hi), row: 8 (over z_lo, core), col: 4 (over y).
Axes of the slice: x: 4, y: 4, z: 8 (z_hi: 2, z_lo: 4; z = z_hi * 4 + z_lo), core: 2. Of those that a mesh axis runs over, the one named last changes fastest.
Arguments:
- traces: bfloat16 [512, 1024, 2048], P(('col', 'row', 'freq')), may hold values from -6 to 6
- band_bins: int32 [256], replicated, may hold values from 1 to 1023
- panel_start: int32 [8], replicated, may hold values from 0 to 7, as said below
Outputs:
- multiples: bfloat16 [2, 256, 1024, 512], P(None, 'freq', 'row', 'col')
Inputs may be any that keep to these rules, and one draw needn't show every extreme that they name: Step n's panel covers shot and receiver indices panel_start[n] * 64 to panel_start[n] * 64 + 63; panels may repeat, and some may be absent.
All inputs are finite; a program needn't handle non-finite values.
Results may differ from a plain program's by a relative error of at most 0.0066.
Values may be sent and summed in bfloat16 or wider, within the bound.
A program may use at most 64 MiB of HBM per device.

v0:
```python
import functools
import math

import jax
import jax.numpy as jnp
from jax import lax
from jax.experimental import pallas as pl
from jax.experimental.pallas import tpu as pltpu
from jax.sharding import PartitionSpec as P

PANEL = 64
MESH = pl.DeviceIdType.MESH
BF16 = jnp.bfloat16
F32 = jnp.float32


def iota(shape, dim):
    return lax.broadcasted_iota(jnp.int32, shape, dim)


def dot(a, b):
    return lax.dot_general(a, b, (((1,), (0,)), ((), ())), preferred_element_type=F32)


def dot_t(a, b):
    return lax.dot_general(a, b, (((1,), (1,)), ((), ())), preferred_element_type=F32)


def cos_sin(phase):
    quadrant = ((phase + 256) >> 9) & 3
    rest = (phase - 512 * ((phase + 256) >> 9)).astype(F32) * (2.0 * math.pi / 2048)
    square = rest * rest
    sine = rest * (1.0 + square * (-1.0 / 6 + square * (1.0 / 120 + square * (-1.0 / 5040 + square * (1.0 / 362880)))))
    cosine = 1.0 + square * (-0.5 + square * (1.0 / 24 + square * (-1.0 / 720 + square * (1.0 / 40320 - square * (1.0 / 3628800)))))
    odd = (quadrant & 1) == 1
    first, second = jnp.where(odd, sine, cosine), jnp.where(odd, cosine, sine)
    first = jnp.where((quadrant == 1) | (quadrant == 2), -first, first)
    second = jnp.where(quadrant >= 2, -second, second)
    return first, second


def kernel(bins_in, starts_in, traces, out, bins, starts, x_buf, table, tiles, send, received, field, left, blocks,
           load_sem, small_sem, send_sem, recv_sem, own_sem, ready_sem):
    f, r, y = (lax.axis_index(n) for n in ("freq", "row", "col"))
    x, zh, zl, core = f // 2, f % 2, r // 2, r % 2
    z = zh * 4 + zl

    def device(x, y, z, core):
        return (x * 2 + z // 4, z % 4 * 2 + core, y)

    barrier = pltpu.get_barrier_semaphore()

    def along_z(k):
        return device(x, y, (z + k // 2) % 8, (core + k % 2) % 2)

    def along_xy(k):
        return device((x + k // 4) % 4, (y + k % 4) % 4, z, core)

    for k in range(1, 16):
        pl.semaphore_signal(barrier, inc=1, device_id=along_z(k), device_id_type=MESH)
    for k in range(1, 16):
        pl.semaphore_signal(barrier, inc=1, device_id=along_xy(k), device_id_type=MESH)

    copy_bins = pltpu.make_async_copy(bins_in, bins, small_sem.at[0])
    copy_starts = pltpu.make_async_copy(starts_in, starts, small_sem.at[1])
    copy_bins.start()

    def load(n):
        return pltpu.make_async_copy(
            traces.at[n // 2, pl.ds(n % 2 * 512, 512)],
            x_buf.at[pl.ds(pl.multiple_of(n * 512, 512), 512)],
            load_sem.at[n],
        )

    for n in range(4):
        load(n).start()
    copy_starts.start()

    row, col = iota((256, 256), 0), iota((256, 256), 1)
    outward = (col == (row & 15) * 16 + ((row >> 4) & 1) * 8 + (row >> 5)).astype(BF16)
    inward = (
        col == ((row >> 1) & 7) * 32 + (row >> 7) * 16 + (row & 1) * 8 + ((row >> 4) & 7)
    ).astype(BF16)

    lane, sub = iota((8, 128), 1), iota((8, 128), 0)

    def build(q):
        half = (core + 1 + q // 2) % 2

        def body(b, _):
            value = jnp.zeros((8, 128), jnp.int32)
            for u in range(8):
                to_y = (y + q % 2 * 2 + u // 4) % 4
                value = jnp.where(sub == u, bins[b * 32 + half * 16 + to_y * 4 + u % 4], value)
            c0, s0 = cos_sin((value * lane) & 2047)
            c1, s1 = cos_sin(((value * lane) & 15) * 128)
            rows = pl.ds(pl.multiple_of(b * 16, 16), 16)
            for u in range(16):
                ca = jnp.broadcast_to(c1[:, u:u + 1], (8, 128))
                sa = jnp.broadcast_to(s1[:, u:u + 1], (8, 128))
                both = jnp.concatenate([c0 * ca - s0 * sa, -(s0 * ca + c0 * sa)], axis=0)
                table[rows, u * 128:(u + 1) * 128] = both.astype(BF16)
            return 0

        lax.fori_loop(0, 8, body, 0, unroll=2)

    def transform(n):
        part = x_buf[pl.ds(pl.multiple_of(n * 512, 512), 512), :]
        spectrum = (dot_t(table[...], part) * (1.0 / math.sqrt(2048))).astype(BF16)
        for u in range(4):
            for b in range(8):
                tiles[pl.ds(pl.multiple_of(n * 64 + u * 16, 16), 16), b * 128:(b + 1) * 128] = (
                    spectrum[b * 16:(b + 1) * 16, u * 128:(u + 1) * 128]
                )

    def pack(q):
        for n in range(4):
            part = dot(outward, tiles[:, n * 256:(n + 1) * 256]).astype(BF16)
            for u in range(2):
                for j in range(8):
                    send[q * 64 + n * 16 + u * 8 + j] = part[j * 32:(j + 1) * 32, u * 128:(u + 1) * 128]

    mine = y * 64 + r * 8 + f

    def spread(q, k):
        to_x, to_y = (x + (k // 8 % 4)) % 4, (y + q % 2 * 2 + (k // 32 % 2)) % 4
        to_z = (z + (k // 1 % 4) + (k // 4 % 2) * 4) % 8
        place = q * 64 + (to_x * 2 + to_z // 4) * 8 + (k // 32 % 2) * 4 + to_z % 4
        return place, device(to_x, to_y, to_z, (core + 1 + q // 2) % 2)

    def push(q):
        def body(k, _):
            place, target = spread(q, k)
            pltpu.make_async_remote_copy(
                src_ref=send.at[place], dst_ref=received.at[mine], send_sem=send_sem.at[0],
                recv_sem=recv_sem.at[q * 4 + (k // 1 % 4)], device_id=target, device_id_type=MESH,
            ).start()
            return 0

        lax.fori_loop(jnp.where(q == 2, 1, 0), 64, body, 0)

    copy_bins.wait()
    build(0)
    for n in range(1):
        load(n).wait()
        transform(n)
    pl.semaphore_wait(barrier, 30)

    for k in range(1, 16):
        pl.semaphore_signal(ready_sem, inc=1, device_id=along_xy(k), device_id_type=MESH)
    for n in range(1, 4):
        load(n).wait()
        transform(n)
    pack(0)
    pl.semaphore_wait(ready_sem, 15)
    push(0)

    def quarter(q, _):
        def body(n, _):
            transform(n)
            return 0

        build(q)
        lax.fori_loop(0, 4, body, 0)
        pack(q)
        push(q)
        return 0

    lax.fori_loop(1, 4, quarter, 0)
    place, _ = spread(2, 0)
    own = pltpu.make_async_copy(send.at[place], received.at[mine], own_sem.at[0])
    own.start()

    copy_starts.wait()
    lane = iota((16, 512), 1)
    weight = jnp.zeros((16, 512), F32)
    for n in range(8):
        weight = weight + jnp.where(lane >> 6 == starts[n], 1.0, 0.0)

    def unpack(g):
        q = g // 4
        from_r = (zl + 4 - g % 4) % 4 * 2 + (core + 1 + q // 2) % 2
        block = [(y + 8 - q % 2 * 2 - u) % 4 * 8 + from_r for u in range(2)]
        if g == 8:
            own.wait()
        arrived = received.at[pl.ds(0, 15 if g == 8 else 16)]
        pltpu.make_async_copy(arrived, arrived, recv_sem.at[g]).wait()
        part = jnp.concatenate(
            [received[pl.ds(block[u] * 8, 8)].reshape(256, 128) for u in range(2)], axis=1
        )
        part = dot(inward, part)
        for u in range(2):
            first = block[u] * 16
            upper, lower = pl.ds(pl.multiple_of(first, 16), 16), pl.ds(pl.multiple_of(512 + first, 16), 16)
            for c in range(2):
                for i in range(8):
                    value = part[(c * 8 + i) * 16:(c * 8 + i + 1) * 16, u * 128:(u + 1) * 128]
                    field[lower if c else upper, i * 128:(i + 1) * 128] = value.astype(BF16)
                    if i < 4:
                        value = value * weight[:, i * 128:(i + 1) * 128]
                        one, two = slice(i * 128, (i + 1) * 128), slice(512 + i * 128, 512 + (i + 1) * 128)
                        if c == 0:
                            left[upper, one] = value.astype(BF16)
                            left[lower, two] = value.astype(BF16)
                        else:
                            left[lower, one] = value.astype(BF16)
                            left[upper, two] = (-value).astype(BF16)

    for g in range(16):
        unpack(g)

    entry = core * 16 + y * 4 + zl

    def multiply(t):
        to_zl = jnp.where(t == 0, (zl + 2) % 4, jnp.where(t == 1, 3 - zl, jnp.where(t == 2, zl + 1 - zl % 2 * 2, zl)))
        lanes = pl.ds(pl.multiple_of(to_zl * 256, 256), 256)
        for part in range(4):
            c, pair = part // 2, part % 2
            rows = slice(part * 256, (part + 1) * 256)
            sums = dot(left[rows, :], field[:, lanes]) * (1.0 / math.sqrt(512))
            turned = sums.astype(BF16).T
            for to_core in range(2):
                for u in range(2):
                    blocks[t * 16 + c * 8 + to_core * 4 + pair * 2 + u] = (
                        turned[to_core * 128:(to_core + 1) * 128, u * 128:(u + 1) * 128]
                    )

            def body(k, _):
                to_core, to_y = k % 2, pair * 2 + k // 2

                @pl.when((t < 3) | (to_core != core) | (to_y != y))
                def _():
                    pltpu.make_async_remote_copy(
                        src_ref=blocks.at[t * 16 + c * 8 + to_core * 4 + to_y], dst_ref=out.at[c, entry],
                        send_sem=send_sem.at[1], recv_sem=recv_sem.at[16],
                        device_id=(f, to_zl * 2 + to_core, to_y), device_id_type=MESH,
                    ).start()

                return 0

            lax.fori_loop(0, 4, body, 0)

    def step(t, _):
        multiply(t)
        return 0

    lax.fori_loop(0, 3, step, 0)
    multiply(3)
    last = [
        pltpu.make_async_copy(blocks.at[48 + c * 8 + core * 4 + y], out.at[c, entry], own_sem.at[1 + c])
        for c in range(2)
    ]
    for c in range(2):
        last[c].start()

    sent = send.at[pl.ds(0, 255)]
    pltpu.make_async_copy(sent, sent, send_sem.at[0]).wait()
    for c in range(2):
        last[c].wait()
    sent = blocks.at[pl.ds(0, 62)]
    pltpu.make_async_copy(sent, sent, recv_sem.at[16]).wait()
    pltpu.make_async_copy(sent, sent, send_sem.at[1]).wait()


def on_device(traces, band_bins, panel_start):
    return pl.pallas_call(
        kernel,
        out_shape=jax.ShapeDtypeStruct((2, 32, 128, 128), BF16),
        in_specs=[
            pl.BlockSpec(memory_space=pl.ANY),
            pl.BlockSpec(memory_space=pl.ANY),
            pl.BlockSpec(memory_space=pl.ANY),
        ],
        out_specs=pl.BlockSpec(memory_space=pltpu.VMEM),
        scratch_shapes=[
            pltpu.SMEM((256,), jnp.int32),
            pltpu.SMEM((8,), jnp.int32),
            pltpu.VMEM((2048, 2048), BF16),
            pltpu.VMEM((128, 2048), BF16),
            pltpu.VMEM((256, 1024), BF16),
            pltpu.VMEM((256, 32, 128), BF16),
            pltpu.VMEM((256, 32, 128), BF16),
            pltpu.VMEM((1024, 1024), BF16),
            pltpu.VMEM((1024, 1024), BF16),
            pltpu.VMEM((64, 128, 128), BF16),
            pltpu.SemaphoreType.DMA((4,)),
            pltpu.SemaphoreType.DMA((2,)),
            pltpu.SemaphoreType.DMA((2,)),
            pltpu.SemaphoreType.DMA((17,)),
            pltpu.SemaphoreType.DMA((3,)),
            pltpu.SemaphoreType.REGULAR,
        ],
        compiler_params=pltpu.CompilerParams(
            collective_id=0, has_side_effects=True, vmem_limit_bytes=48 * 2**20
        ),
        cost_estimate=pl.CostEstimate(flops=9_000_000_000, bytes_accessed=10 * 2**20, transcendentals=0),
        name="multiples",
    )(*(pltpu.with_memory_space_constraint(v, pltpu.HBM) for v in (band_bins, panel_start, traces)))


def solution(mesh):
    return jax.shard_map(
        on_device,
        mesh=mesh,
        in_specs=(P(("col", "row", "freq"), None, None), P(), P()),
        out_specs=P(None, "freq", "row", "col"),
        check_vma=False,
    )
```

profile of v0, /device:TPU:57, one launch (start us, length us, event | category | flops | bytes accessed | tf_op | source)
XLA Modules:
  0.0 109.2 jit_solution(8675481995197762702)
XLA Ops:
  0.0 107.9 %multiples.1 = bf16[2,32,128,128]{3,2,1,0:T(8,128)(2,1)S(1)} custom-call(s32[256]{0:T(256)} %bins_in.1, s32[8]{0:T(128)} %starts_in.1, bf16[2,1024,2048]{2,1,0:T(8,128)(2,1)} %traces.1), custom_call_target="tpu_custom_call" | custom-call | flops 8999999488 | bytes 10485760 | tf_op jit(solution)/shard_map/multiples/pallas_call | solution.py:266
  107.9 1.3 %copy.5 = bf16[2,32,128,128]{3,2,1,0:T(8,128)(2,1)} copy(bf16[2,32,128,128]{3,2,1,0:T(8,128)(2,1)S(1)} %multiples.1) | data formatting | bytes 4194304
where the time goes:
time: 109 us
  Pallas kernels  108 us (99%)
  local copies, waits for them, and re-layouts  1.32 us (1%)
    pallas_call x1, Pallas kernels, on_device(): pl.pallas_call(kernel, out_shape=jax.ShapeDtypeStruct((2, 32, 128, 128),...  108 us

commit v1 on v0

--- a/solution.py
+++ b/solution.py
@@ -215,8 +215,8 @@
         to_zl = jnp.where(t == 0, (zl + 2) % 4, jnp.where(t == 1, 3 - zl, jnp.where(t == 2, zl + 1 - zl % 2 * 2, zl)))
         lanes = pl.ds(pl.multiple_of(to_zl * 256, 256), 256)
         for part in range(4):
-            c, pair = part // 2, part % 2
-            rows = slice(part * 256, (part + 1) * 256)
+            c, pair = part // 2, (part + 1 + y // 2) % 2
+            rows = pl.ds(pl.multiple_of(c * 512 + pair * 256, 256), 256)
             sums = dot(left[rows, :], field[:, lanes]) * (1.0 / math.sqrt(512))
             turned = sums.astype(BF16).T
             for to_core in range(2):

time: 109 us -> 109 us (level)
  no operation moved by 1% of the time
where the time goes in v1:
time: 109 us
  Pallas kernels  107 us (98%)
  local copies, waits for them, and re-layouts  1.32 us (1%)
    pallas_call x1, Pallas kernels, on_device(): pl.pallas_call(kernel, out_shape=jax.ShapeDtypeStruct((2, 32, 128, 128),...  107 us

profile of v1, /device:TPU:57, one launch (start us, length us, event | category | flops | bytes accessed | tf_op | source)
XLA Modules:
  0.0 108.6 jit_solution(8831261833999603537)
XLA Ops:
  0.0 107.2 %multiples.1 = bf16[2,32,128,128]{3,2,1,0:T(8,128)(2,1)S(1)} custom-call(s32[256]{0:T(256)} %bins_in.1, s32[8]{0:T(128)} %starts_in.1, bf16[2,1024,2048]{2,1,0:T(8,128)(2,1)} %traces.1), custom_call_target="tpu_custom_call" | custom-call | flops 8999999488 | bytes 10485760 | tf_op jit(solution)/shard_map/multiples/pallas_call | solution.py:266
  107.2 1.3 %copy.5 = bf16[2,32,128,128]{3,2,1,0:T(8,128)(2,1)} copy(bf16[2,32,128,128]{3,2,1,0:T(8,128)(2,1)S(1)} %multiples.1) | data formatting | bytes 4194304
